TPU v7x, 32 devices: a whole 2x2x4 slice. The times are simulated.
32 devices in a mesh: groups: 2 (over y), ha: 4 (over z), ta: 2 (over x), col: 2 (over core).
Axes of the slice: x: 2, y: 2, z: 4, core: 2. Of those that a mesh axis runs over, the one named last changes fastest.
Arguments:
- tokens: bfloat16 [8, 16, 64, 768], P(('groups', 'ta'), 'ha', None, 'col'), parts along dimension 0, may hold values from -6 to 6
- norm1_gain: float32 [768], replicated, may hold values from 0.4 to 1.6
- w_qkv: bfloat16 [3, 768, 768], P(None, None, 'col'), may hold values from -0.21875 to 0.21875
- w_out: bfloat16 [768, 768], P('col'), may hold values from -0.3125 to 0.3125
- norm2_gain: float32 [768], replicated, may hold values from 0.4 to 1.6
- w_up: bfloat16 [768, 3072], P('ha', 'col'), may hold values from -0.21875 to 0.21875
- w_down: bfloat16 [3072, 768], P('col', 'ha'), may hold values from -0.109375 to 0.109375
Outputs:
- block_out: bfloat16 [8, 16, 64, 768], P(('groups', 'ta'), 'ha', None, 'col'), parts along dimension 0
There are 2 independent parts, one for each index of `groups`. A program takes and returns all parts, laid end to end along the dimension named above; an argument that names none is the same for every part. Nothing has to cross between parts.
All inputs are finite; a program needn't handle non-finite values.
Results may differ from a plain program's by a relative error of at most 0.009.
Values may be sent and summed in bfloat16 or wider, within the bound.
A program may use at most 64 MiB of HBM per device.

v0:
```python
import math
import jax
import jax.numpy as jnp
from jax import lax
from jax.sharding import PartitionSpec as P

HD = 64
EPS = 1e-05


def layer_norm(values, gain):
    mean = jnp.mean(values, -1, keepdims=True)
    centred = values - mean
    spread = jnp.mean(centred * centred, -1, keepdims=True)
    return centred * lax.rsqrt(spread + EPS) * gain


def attend(query, keys, values, dim):
    scale = 1.0 / math.sqrt(HD)
    moved_q = jnp.moveaxis(query, dim, -2)
    moved_k = jnp.moveaxis(keys, dim, -2)
    moved_v = jnp.moveaxis(values, dim, -2)
    shape = moved_q.shape
    split = shape[:-1] + (shape[-1] // HD, HD)
    scores = (
        jnp.einsum(
            "...qhd,...khd->...hqk",
            moved_q.reshape(split),
            moved_k.reshape(split),
            preferred_element_type=jnp.float32,
        )
        * scale
    )
    weights = jnp.exp(scores)
    weights = (weights / jnp.sum(weights, -1, keepdims=True)).astype(jnp.bfloat16)
    result = jnp.einsum(
        "...hqk,...khd->...qhd", weights, moved_v.reshape(split), preferred_element_type=jnp.float32
    ).astype(jnp.bfloat16)
    return jnp.moveaxis(result.reshape(shape), -2, dim)


def on_device(tokens, norm1_gain, w_qkv, w_out, norm2_gain, w_up, w_down):
    whole = lax.all_gather(tokens, "col", axis=3, tiled=True)
    frames, rows_h, width, model = whole.shape
    count = frames * rows_h * width
    half = tokens.shape[3]
    wide = whole.astype(jnp.float32).reshape(count, model)
    normed = layer_norm(wide, norm1_gain).astype(jnp.bfloat16)
    stacked = jnp.einsum("rd,sdc->src", normed, w_qkv, preferred_element_type=jnp.float32).astype(
        jnp.bfloat16
    )
    stacked = stacked.reshape(3, frames, rows_h, width, half)
    along_w = attend(stacked[0], stacked[1], stacked[2], 2)
    columns = lax.all_to_all(stacked, "ha", split_axis=3, concat_axis=2, tiled=True)
    along_h_far = attend(columns[0], columns[1], columns[2], 1)
    along_h = lax.all_to_all(along_h_far, "ha", split_axis=1, concat_axis=2, tiled=True)
    lines = lax.all_to_all(stacked, "ta", split_axis=3, concat_axis=1, tiled=True)
    along_t_far = attend(lines[0], lines[1], lines[2], 0)
    along_t = lax.all_to_all(along_t_far, "ta", split_axis=0, concat_axis=2, tiled=True)
    mixed = (
        along_w.astype(jnp.float32) + along_h.astype(jnp.float32) + along_t.astype(jnp.float32)
    ).astype(jnp.bfloat16)
    terms = jnp.dot(mixed.reshape(count, half), w_out, preferred_element_type=jnp.float32)
    offset = lax.axis_index("col") * half
    summed = lax.psum(terms, "col")
    first_full = wide + summed
    second = layer_norm(first_full, norm2_gain).astype(jnp.bfloat16)
    first = lax.dynamic_slice_in_dim(first_full, offset, half, 1)
    upper = jnp.dot(
        second, lax.all_gather(w_up, "ha", axis=0, tiled=True), preferred_element_type=jnp.float32
    )
    hidden = jax.nn.gelu(upper, approximate=False).astype(jnp.bfloat16)
    down_terms = jnp.dot(
        hidden, lax.all_gather(w_down, "ha", axis=1, tiled=True), preferred_element_type=jnp.float32
    )
    down_share = lax.psum_scatter(
        down_terms.astype(jnp.bfloat16), "col", scatter_dimension=1, tiled=True
    ).astype(jnp.float32)
    return (first + down_share).astype(jnp.bfloat16).reshape(frames, rows_h, width, half)


def solution(mesh):
    placed = (
        P(("groups", "ta"), "ha", None, "col"),
        P(),
        P(None, None, "col"),
        P("col", None),
        P(),
        P("ha", "col"),
        P("col", "ha"),
    )
    return jax.shard_map(
        on_device,
        mesh=mesh,
        in_specs=placed,
        out_specs=P(("groups", "ta"), "ha", None, "col"),
        check_vma=False,
    )
```

profile of v0, /device:TPU:0, one launch (start us, length us, event | category | flops | bytes accessed | tf_op | source)
XLA Modules:
  0.0 270.8 jit_solution(178408443112723178)
XLA Ops:
  7.4 2.8 %all_gather.9 = bf16[2,4,64,768]{3,2,1,0:T(8,128)(2,1)S(1)} all-gather(bf16[2,4,64,384]{3,2,1,0:T(8,128)(2,1)} %param.7), channel_id=1, replica_groups=mesh['groups'=2,'ha'=4,'ta'=2,'col'=2] {'col'}, dimensions={3}, use_global_device_ids=true | all-gather | bytes 1179648 | tf_op jit(solution)/shard_map/all_gather | solution.py:43
  15.4 19.9 %all_to_all.48 = bf16[3,2,4,64,384]{4,2,1,0,3:T(4,128)(2,1)} all-to-all(bf16[3,2,4,64,384]{4,2,1,0,3:T(4,128)(2,1)S(1)} %copy.127), channel_id=1, replica_groups=mesh['groups'=2,'ha'=4,'ta'=2,'col'=2] {'ta'}, dimensions={3} | all-to-all | bytes 2359296 | tf_op jit(solution)/shard_map/all_to_all | solution.py:57
  35.3 5.1 %all-to-all-start = ((bf16[3,2,4,64,384]{4,2,1,0,3:T(4,128)(2,1)}), bf16[3,2,4,64,384]{4,2,1,0,3:T(4,128)(2,1)}, u32[]{:S(2)}, u32[]{:S(2)}) async-start(bf16[3,2,4,64,384]{4,2,1,0,3:T(4,128)(2,1)} %copy-done.1), calls=%async_computation | async-start | bytes 2359296 | tf_op jit(solution)/shard_map/all_to_all | solution.py:54
  42.5 2.4 reshape.133
  49.6 2.4 reshape.139
  56.2 3.9 %fusion.23 = f32[4,32,6,4,4]{3,4,2,1,0:T(4,128)} fusion(bf16[4,32,4,6,64]{4,3,1,0,2:T(8,128)(2,1)} %reshape.140, bf16[4,32,4,6,64]{4,3,1,0,2:T(8,128)(2,1)} %reshape.139), kind=kOutput, calls=%fused_computation.46 | convolution fusion | flops 1572864 | bytes 835584 | tf_op jit(solution)/shard_map/...qhd,...khd->...hqk/dot_general | solution.py:26
  68.4 2.4 fusion.21
  74.7 4.4 %all-to-all-start.3 = ((bf16[4,4,32,384]{3,2,1,0:T(8,128)(2,1)}), bf16[4,4,32,384]{3,2,1,0:T(8,128)(2,1)}, u32[]{:S(2)}, u32[]{:S(2)}) async-start(bf16[4,4,32,384]{3,2,1,0:T(8,128)(2,1)} %copy.158), calls=%async_computation.3 | async-start | bytes 786432 | tf_op jit(solution)/shard_map/all_to_all | solution.py:59
  86.4 2.4 reshape.137
  89.6 2.4 reshape.135
  92.1 3.8 %multiply_exponential_fusion = f32[2,16,6,16,16]{3,4,2,1,0:T(8,128)} fusion(bf16[2,16,16,6,64]{4,3,1,2,0:T(8,128)(2,1)} %reshape.137, bf16[2,16,16,6,64]{4,3,1,2,0:T(8,128)(2,1)} %reshape.136), kind=kOutput, calls=%fused_computation.32 | convolution fusion | flops 6340608 | bytes 983040 | tf_op jit(solution)/shard_map/...qhd,...khd->...hqk/dot_general | solution.py:26
  95.9 3.9 %fusion.20 = bf16[2,16,16,6,64]{4,2,3,1,0:T(8,128)(2,1)} fusion(f32[2,16,6,16,16]{3,4,2,1,0:T(8,128)} %multiply_exponential_fusion, bf16[2,16,16,6,64]{4,3,1,2,0:T(8,128)(2,1)} %reshape.135), kind=kOutput, calls=%fused_computation.41 | convolution fusion | flops 6589455 | bytes 983040 | tf_op jit(solution)/shard_map/...hqk,...khd->...qhd/dot_general | solution.py:36
  104.9 5.1 %all-to-all-start.1 = ((bf16[2,16,16,384]{3,2,0,1:T(8,128)(2,1)}), bf16[2,16,16,384]{3,2,0,1:T(8,128)(2,1)}, u32[]{:S(2)}, u32[]{:S(2)}) async-start(bf16[2,16,16,384]{3,2,0,1:T(8,128)(2,1)} %copy.140), calls=%async_computation.1 | async-start | bytes 786432 | tf_op jit(solution)/shard_map/all_to_all | solution.py:56
  110.0 3.3 %multiply_exponential_fusion.1 = f32[2,4,6,64,64]{3,4,2,1,0:T(8,128)} fusion(bf16[2,4,64,6,64]{4,3,2,1,0:T(8,128)(2,1)} %reshape.134, bf16[2,4,64,6,64]{4,3,2,1,0:T(8,128)(2,1)} %reshape.133), kind=kOutput, calls=%fused_computation.34 | convolution fusion | flops 25362432 | bytes 1572864 | tf_op jit(solution)/shard_map/...qhd,...khd->...hqk/dot_general | solution.py:26
  114.8 3.8 %convert_bitcast_fusion = f32[2,4,64,6,64]{2,4,3,1,0:T(8,128)} fusion(f32[2,4,6,64,64]{3,4,2,1,0:T(8,128)} %multiply_exponential_fusion.1, bf16[2,4,64,6,64]{4,3,2,1,0:T(8,128)(2,1)} %reshape.132), kind=kOutput, calls=%fused_computation.28 | convolution fusion | flops 25955392 | bytes 1966080 | tf_op jit(solution)/shard_map/...hqk,...khd->...qhd/dot_general | solution.py:36
  118.6 3.6 %copy.126 = f32[2,4,64,6,64]{2,1,0,4,3:T(4,128)} copy(f32[2,4,64,6,64]{2,4,3,1,0:T(8,128)} %convert_bitcast_fusion) | data formatting | bytes 1572864 | tf_op jit(solution)/shard_map/convert_element_type | solution.py:61
  122.2 3.1 %reshape.126 = f32[512,384]{0,1:T(8,128)} reshape(f32[2,4,64,6,64]{2,1,0,4,3:T(4,128)} %copy.126) | data formatting | bytes 1572864 | tf_op jit(solution)/shard_map/convert_element_type | solution.py:61
  130.0 3.6 %fusion.44 = f32[512,768]{1,0:T(8,128)} fusion(bf16[384,768]{1,0:T(8,128)(2,1)} %param.10, f32[512,384]{0,1:T(8,128)} %copy.160, f32[512,384]{0,1:T(8,128)} %reshape.126, f32[512,384]{0,1:T(8,128)} %copy.143), kind=kOutput, calls=%fused_computation.64 | convolution fusion | flops 302579712 | bytes 4521984 | tf_op jit(solution)/shard_map/dot_general | solution.py:63
  135.1 20.9 %all-reduce.2.cloned.1.call-done = f32[512,768]{1,0:T(8,128)} async-done(((f32[512,768]{1,0:T(8,128)}), f32[512,768]{1,0:T(8,128)}) %all-reduce.2.cloned.1.call-update) | async-done | bytes 1572880 | tf_op jit(solution)/shard_map/psum | solution.py:65
  159.1 28.4 %all-gather.3.cloned.1.call-done = bf16[768,1536]{1,0:T(8,128)(2,1)} async-done(((bf16[192,1536]{1,0:T(8,128)(2,1)}), bf16[768,1536]{1,0:T(8,128)(2,1)}) %all-gather.3.cloned.1.call-update) | async-done | bytes 2359312 | tf_op jit(solution)/shard_map/all_gather | solution.py:70
  187.6 50.3 %all-gather.5.cloned.1.call-done = bf16[1536,768]{0,1:T(8,128)(2,1)} async-done(((bf16[1536,192]{0,1:T(8,128)(2,1)}), bf16[1536,768]{0,1:T(8,128)(2,1)}) %all-gather.5.cloned.1.call-update) | async-done | bytes 2359312 | tf_op jit(solution)/shard_map/all_gather | solution.py:74
  237.8 12.3 %fusion.17 = bf16[512,768]{1,0:T(8,128)(2,1)} fusion(bf16[1536,768]{0,1:T(8,128)(2,1)} %all-gather.5.cloned.1.call-done, bf16[768,1536]{1,0:T(8,128)(2,1)} %all-gather.3.cloned.1.call-done, f32[512,768]{1,0:T(8,128)} %copy-done.2, f32[768]{0:T(1024)S(1)} %copy-done.6, f32[512]{0:T(512)S(1)} %add_rsqrt_fusion.1, f32[512]{0:T(512)S(1)} %broadcast_multiply_fusion.1), kind=kOutput, calls=%fused_computation.37 | convolution fusion | flops 2469003264 | bytes 7085056 | tf_op jit(solution)/shard_map/dot_general | solution.py:73
  250.1 2.4 copy.181
  252.6 7.0 %reduce-scatter.4.cloned.1.call-done = bf16[384,512]{1,0:T(8,128)(2,1)} async-done(((bf16[768,512]{1,0:T(8,128)(2,1)}), bf16[384,512]{1,0:T(8,128)(2,1)}) %reduce-scatter.4.cloned.1.call-update) | async-done | bytes 393232
  (73 shorter events, 56.0 us)
Async XLA Ops:
  7.4 3.8 %copy-start = (bf16[3,768,384]{2,1,0:T(8,128)(2,1)S(1)}, bf16[3,768,384]{2,1,0:T(8,128)(2,1)}, u32[]{:S(2)}) copy-start(bf16[3,768,384]{2,1,0:T(8,128)(2,1)} %param.9) | copy-start | bytes 5308420
  7.4 3.5 %copy-start.5 = (f32[768]{0:T(1024)S(1)}, f32[768]{0:T(1024)}, u32[]{:S(2)}) copy-start(f32[768]{0:T(1024)} %param.8) | copy-start | bytes 9220
  12.4 1.0 copy-start.4
  14.4 1.0 copy-start.1
  35.3 39.4 %all-to-all-start = ((bf16[3,2,4,64,384]{4,2,1,0,3:T(4,128)(2,1)}), bf16[3,2,4,64,384]{4,2,1,0,3:T(4,128)(2,1)}, u32[]{:S(2)}, u32[]{:S(2)}) async-start(bf16[3,2,4,64,384]{4,2,1,0,3:T(4,128)(2,1)} %copy-done.1), calls=%async_computation | async-start | bytes 2359296 | tf_op jit(solution)/shard_map/all_to_all | solution.py:54
  74.7 30.2 %all-to-all-start.3 = ((bf16[4,4,32,384]{3,2,1,0:T(8,128)(2,1)}), bf16[4,4,32,384]{3,2,1,0:T(8,128)(2,1)}, u32[]{:S(2)}, u32[]{:S(2)}) async-start(bf16[4,4,32,384]{3,2,1,0:T(8,128)(2,1)} %copy.158), calls=%async_computation.3 | async-start | bytes 786432 | tf_op jit(solution)/shard_map/all_to_all | solution.py:59
  104.9 22.8 %all-to-all-start.1 = ((bf16[2,16,16,384]{3,2,0,1:T(8,128)(2,1)}), bf16[2,16,16,384]{3,2,0,1:T(8,128)(2,1)}, u32[]{:S(2)}, u32[]{:S(2)}) async-start(bf16[2,16,16,384]{3,2,0,1:T(8,128)(2,1)} %copy.140), calls=%async_computation.1 | async-start | bytes 786432 | tf_op jit(solution)/shard_map/all_to_all | solution.py:56
  110.0 46.1 %all-reduce.2.cloned.1.call-start = ((), (), s32[]{:S(2)}) async-start(), calls=%async_computation.5 | async-start | bytes 3145728 | tf_op jit(solution)/shard_map/psum | solution.py:65
  133.7 53.9 %all-gather.3.cloned.1.call-start = ((), (), s32[]{:S(2)}) async-start(), calls=%async_computation.6 | async-start | bytes 2949120 | tf_op jit(solution)/shard_map/all_gather | solution.py:70
  134.2 103.6 %all-gather.5.cloned.1.call-start = ((), (), s32[]{:S(2)}) async-start(), calls=%async_computation.7 | async-start | bytes 2949120 | tf_op jit(solution)/shard_map/all_gather | solution.py:74
  134.8 103.0 %copy-start.6 = (f32[768]{0:T(1024)S(1)}, f32[768]{0:T(1024)}, u32[]{:S(2)}) copy-start(f32[768]{0:T(1024)} %param.11) | copy-start | bytes 9220
  134.8 124.8 %reduce-scatter.4.cloned.1.call-start = ((), (), s32[]{:S(2)}) async-start(), calls=%async_computation.8 | async-start | bytes 1179648
  157.7 1.2 copy-start.2
  250.1 11.4 %copy-start.3 = (f32[512,768]{1,0:T(8,128)S(1)}, f32[512,768]{1,0:T(8,128)}, u32[]{:S(2)}) copy-start(f32[512,768]{1,0:T(8,128)} %copy-done.2) | copy-start | bytes 4718596
Sparse Core Ops, SparseCore 0:
  133.8 22.2 all-reduce.1
  252.7 6.8 reduce-scatter.3
Sparse Core Ops, SparseCore 1:
  135.8 51.7 all-gather.2
  189.1 48.7 all-gather.4
where the time goes:
time: 272 us; the launch traced here: 271 us
  waiting for transfers between devices  108 us (40%)
  local copies, waits for them, and re-layouts  65.5 us (24%)
  matrix products  38.2 us (14%)
  blocking collectives  22.7 us (8%)
  between operations  15 us (6%)
  starting transfers between devices  14.9 us (5%)
  other arithmetic  6.71 us (2%)
    all_gather x1, waiting for transfers between devices, on_device(): lax.all_gather(w_down, 'ha', axis=1, tiled=True)  50.3 us
    all_gather x1, waiting for transfers between devices, on_device(): lax.all_gather(w_up, 'ha', axis=0, tiled=True)  28.4 us
    psum x1, waiting for transfers between devices, on_device(): summed = lax.psum(terms, 'col')  20.9 us
    all_to_all x1, blocking collectives, on_device(): lax.all_to_all(stacked, 'ta', split_axis=3, concat_axis=1, tiled=True)  19.9 us
    dot_general x1, matrix products, on_device(): jnp.dot(hidden, lax.all_gather(w_down, 'ha', axis=1, tiled=True), preferr...  12.3 us
    dot_general x3, matrix products, attend(): jnp.einsum('...qhd,...khd->...hqk', moved_q.reshape(split), moved_k.resha...  10.9 us
    dot_general x3, matrix products, attend(): jnp.einsum('...hqk,...khd->...qhd', weights, moved_v.reshape(split), pref...  10.2 us
    unnamed x5, waiting for transfers between devices  8.13 us
  transfers between devices with their start and end apart: 7, of which 4 were waited for; matrix products, arithmetic and copies ran while one was open for 29% of the time, Pallas kernels for 0%

commit v1 on v0

--- a/solution.py
+++ b/solution.py
@@ -62,7 +62,8 @@
     ).astype(jnp.bfloat16)
     terms = jnp.dot(mixed.reshape(count, half), w_out, preferred_element_type=jnp.float32)
     offset = lax.axis_index("col") * half
-    summed = lax.psum(terms, "col")
+    shards = lax.all_gather(terms, "col")
+    summed = jnp.sum(shards, axis=0)
     first_full = wide + summed
     second = layer_norm(first_full, norm2_gain).astype(jnp.bfloat16)
     first = lax.dynamic_slice_in_dim(first_full, offset, half, 1)

time: 272 us -> 282 us (1.037)
  other arithmetic: 6.71 us -> 14.6 us
  waiting for transfers between devices: 108 us -> 115 us
  local copies, waits for them, and re-layouts: 65.5 us -> 62.4 us
    psum x1 -> x0, waiting for transfers between devices: 20.9 us -> none  [on_device(): summed = lax.psum(terms, 'col')]
    all_gather x1, waiting for transfers between devices: 28.4 us -> 43.4 us  [on_device(): lax.all_gather(w_up, 'ha', axis=0, tiled=True)]
    all_gather x0 -> x1, waiting for transfers between devices: none -> 12.3 us  [on_device(): shards = lax.all_gather(terms, 'col')]
    reduce_sum x0 -> x1, other arithmetic: none -> 3.49 us  [on_device(): summed = jnp.sum(shards, axis=0)]
    unnamed x16 -> x12, local copies, waits for them, and re-layouts: 7.54 us -> 4.43 us
  transfers between devices with their start and end apart: 7 -> 7, of which waited for: 4 -> 4; matrix products, arithmetic and copies ran while one was open for 29% -> 31% of each run, Pallas kernels for 0% -> 0%
where the time goes in v1:
time: 282 us; the launch traced here: 280 us
  waiting for transfers between devices  115 us (41%)
  local copies, waits for them, and re-layouts  62.4 us (22%)
  matrix products  37.3 us (13%)
  blocking collectives  22.7 us (8%)
  starting transfers between devices  14.9 us (5%)
  other arithmetic  14.6 us (5%)
  between operations  13.3 us (5%)
    all_gather x1, waiting for transfers between devices, on_device(): lax.all_gather(w_down, 'ha', axis=1, tiled=True)  50.9 us
    all_gather x1, waiting for transfers between devices, on_device(): lax.all_gather(w_up, 'ha', axis=0, tiled=True)  43.4 us
    all_to_all x1, blocking collectives, on_device(): lax.all_to_all(stacked, 'ta', split_axis=3, concat_axis=1, tiled=True)  19.9 us
    all_gather x1, waiting for transfers between devices, on_device(): shards = lax.all_gather(terms, 'col')  12.3 us
    dot_general x1, matrix products, on_device(): jnp.dot(hidden, lax.all_gather(w_down, 'ha', axis=1, tiled=True), preferr...  11.4 us
    dot_general x3, matrix products, attend(): jnp.einsum('...qhd,...khd->...hqk', moved_q.reshape(split), moved_k.resha...  10.9 us
    dot_general x3, matrix products, attend(): jnp.einsum('...hqk,...khd->...qhd', weights, moved_v.reshape(split), pref...  10.2 us
    unnamed x5, waiting for transfers between devices  8.62 us
  transfers between devices with their start and end apart: 7, of which 4 were waited for; matrix products, arithmetic and copies ran while one was open for 31% of the time, Pallas kernels for 0%

profile of v1, /device:TPU:0, one launch (start us, length us, event | category | flops | bytes accessed | tf_op | source)
XLA Modules:
  0.0 280.4 jit_solution(16418462198487933664)
XLA Ops:
  6.5 2.8 all_gather.15
  14.6 19.9 %all_to_all.48 = bf16[3,2,4,64,384]{4,2,1,0,3:T(4,128)(2,1)} all-to-all(bf16[3,2,4,64,384]{4,2,1,0,3:T(4,128)(2,1)S(1)} %copy.127), channel_id=1, replica_groups=mesh['groups'=2,'ha'=4,'ta'=2,'col'=2] {'ta'}, dimensions={3} | all-to-all | bytes 2359296 | tf_op jit(solution)/shard_map/all_to_all | solution.py:57
  34.5 5.1 %all-to-all-start = ((bf16[3,2,4,64,384]{4,2,1,0,3:T(4,128)(2,1)}), bf16[3,2,4,64,384]{4,2,1,0,3:T(4,128)(2,1)}, u32[]{:S(2)}, u32[]{:S(2)}) async-start(bf16[3,2,4,64,384]{4,2,1,0,3:T(4,128)(2,1)} %copy-done.1), calls=%async_computation | async-start | bytes 2359296 | tf_op jit(solution)/shard_map/all_to_all | solution.py:54
  41.7 2.4 reshape.156
  55.3 3.8 %fusion.24 = f32[4,32,6,4,4]{3,4,2,1,0:T(4,128)} fusion(bf16[4,32,4,6,64]{4,3,1,0,2:T(8,128)(2,1)} %reshape.163, bf16[4,32,4,6,64]{4,3,1,0,2:T(8,128)(2,1)} %reshape.162), kind=kOutput, calls=%fused_computation.48 | convolution fusion | flops 1572864 | bytes 835584 | tf_op jit(solution)/shard_map/...qhd,...khd->...hqk/dot_general | solution.py:26
  65.1 2.4 reshape.161
  67.5 2.4 fusion.21
  73.8 4.3 %all-to-all-start.3 = ((bf16[4,4,32,384]{3,2,1,0:T(8,128)(2,1)}), bf16[4,4,32,384]{3,2,1,0:T(8,128)(2,1)}, u32[]{:S(2)}, u32[]{:S(2)}) async-start(bf16[4,4,32,384]{3,2,1,0:T(8,128)(2,1)} %copy.158), calls=%async_computation.3 | async-start | bytes 786432 | tf_op jit(solution)/shard_map/all_to_all | solution.py:59
  85.5 2.4 reshape.160
  91.0 3.8 %multiply_exponential_fusion = f32[2,16,6,16,16]{3,4,2,1,0:T(8,128)} fusion(bf16[2,16,16,6,64]{4,3,1,2,0:T(8,128)(2,1)} %reshape.160, bf16[2,16,16,6,64]{4,3,1,2,0:T(8,128)(2,1)} %reshape.159), kind=kOutput, calls=%fused_computation.33 | convolution fusion | flops 6340608 | bytes 983040 | tf_op jit(solution)/shard_map/...qhd,...khd->...hqk/dot_general | solution.py:26
  94.8 3.9 %fusion.20 = bf16[2,16,16,6,64]{4,2,3,1,0:T(8,128)(2,1)} fusion(f32[2,16,6,16,16]{3,4,2,1,0:T(8,128)} %multiply_exponential_fusion, bf16[2,16,16,6,64]{4,3,1,2,0:T(8,128)(2,1)} %reshape.158), kind=kOutput, calls=%fused_computation.42 | convolution fusion | flops 6589455 | bytes 983040 | tf_op jit(solution)/shard_map/...hqk,...khd->...qhd/dot_general | solution.py:36
  103.8 5.1 %all-to-all-start.1 = ((bf16[2,16,16,384]{3,2,0,1:T(8,128)(2,1)}), bf16[2,16,16,384]{3,2,0,1:T(8,128)(2,1)}, u32[]{:S(2)}, u32[]{:S(2)}) async-start(bf16[2,16,16,384]{3,2,0,1:T(8,128)(2,1)} %copy.140), calls=%async_computation.1 | async-start | bytes 786432 | tf_op jit(solution)/shard_map/all_to_all | solution.py:56
  108.9 3.2 %multiply_exponential_fusion.1 = f32[2,4,6,64,64]{3,4,2,1,0:T(8,128)} fusion(bf16[2,4,64,6,64]{4,3,2,1,0:T(8,128)(2,1)} %reshape.157, bf16[2,4,64,6,64]{4,3,2,1,0:T(8,128)(2,1)} %reshape.156), kind=kOutput, calls=%fused_computation.35 | convolution fusion | flops 25362432 | bytes 1572864 | tf_op jit(solution)/shard_map/...qhd,...khd->...hqk/dot_general | solution.py:26
  113.7 3.8 %convert_bitcast_fusion = f32[2,4,64,6,64]{2,4,3,1,0:T(8,128)} fusion(f32[2,4,6,64,64]{3,4,2,1,0:T(8,128)} %multiply_exponential_fusion.1, bf16[2,4,64,6,64]{4,3,2,1,0:T(8,128)(2,1)} %reshape.155), kind=kOutput, calls=%fused_computation.29 | convolution fusion | flops 25955392 | bytes 1966080 | tf_op jit(solution)/shard_map/...hqk,...khd->...qhd/dot_general | solution.py:36
  117.6 3.6 %copy.126 = f32[2,4,64,6,64]{2,1,0,4,3:T(4,128)} copy(f32[2,4,64,6,64]{2,4,3,1,0:T(8,128)} %convert_bitcast_fusion) | data formatting | bytes 1572864 | tf_op jit(solution)/shard_map/convert_element_type | solution.py:61
  121.1 3.1 %reshape.148 = f32[512,384]{0,1:T(8,128)} reshape(f32[2,4,64,6,64]{2,1,0,4,3:T(4,128)} %copy.126) | data formatting | bytes 1572864 | tf_op jit(solution)/shard_map/convert_element_type | solution.py:61
  128.9 3.7 %fusion.45 = f32[512,768]{1,0:T(8,128)} fusion(bf16[384,768]{1,0:T(8,128)(2,1)} %param.10, f32[512,384]{0,1:T(8,128)} %copy.160, f32[512,384]{0,1:T(8,128)} %reshape.148, f32[512,384]{0,1:T(8,128)} %copy.143), kind=kOutput, calls=%fused_computation.66 | convolution fusion | flops 302579712 | bytes 4521984 | tf_op jit(solution)/shard_map/dot_general | solution.py:63
  134.4 12.3 %all-gather.9.cloned.1.call-done = f32[1024,768]{1,0:T(8,128)} async-done(((f32[512,768]{1,0:T(8,128)}), f32[1024,768]{1,0:T(8,128)}) %all-gather.9.cloned.1.call-update) | async-done | bytes 3145744 | tf_op jit(solution)/shard_map/all_gather | solution.py:65
  146.7 3.5 %reduce_sum.79 = f32[512,768]{1,0:T(8,128)} reduce(f32[2,512,768]{2,1,0:T(8,128)} %bitcast.103, f32[]{:T(128)} %constant.37.clone.1), dimensions={0}, to_apply=%region_5.0 | reduce | flops 393216 | bytes 4718596 | tf_op jit(solution)/shard_map/reduce_sum | solution.py:66
  153.8 2.8 bitcast_add_fusion
  156.6 43.4 %all-gather.5.cloned.1.call-done = bf16[768,1536]{1,0:T(8,128)(2,1)} async-done(((bf16[192,1536]{1,0:T(8,128)(2,1)}), bf16[768,1536]{1,0:T(8,128)(2,1)}) %all-gather.5.cloned.1.call-update) | async-done | bytes 2359312 | tf_op jit(solution)/shard_map/all_gather | solution.py:71
  200.0 50.9 %all-gather.7.cloned.1.call-done = bf16[1536,768]{0,1:T(8,128)(2,1)} async-done(((bf16[1536,192]{0,1:T(8,128)(2,1)}), bf16[1536,768]{0,1:T(8,128)(2,1)}) %all-gather.7.cloned.1.call-update) | async-done | bytes 2359312 | tf_op jit(solution)/shard_map/all_gather | solution.py:75
  250.9 11.4 %fusion.17 = bf16[512,768]{1,0:T(8,128)(2,1)S(1)} fusion(bf16[1536,768]{0,1:T(8,128)(2,1)} %all-gather.7.cloned.1.call-done, bf16[768,1536]{1,0:T(8,128)(2,1)} %all-gather.5.cloned.1.call-done, f32[512,768]{1,0:T(8,128)} %bitcast_add_fusion, f32[768]{0:T(1024)S(1)} %copy-done.4, f32[512]{0:T(512)S(1)} %rsqrt.25, f32[512]{0:T(512)S(1)} %div.50), kind=kOutput, calls=%fused_computation.38 | convolution fusion | flops 2469003264 | bytes 7085056 | tf_op jit(solution)/shard_map/dot_general | solution.py:74
  263.5 7.2 %reduce-scatter.4.cloned.1.call-done = bf16[384,512]{1,0:T(8,128)(2,1)} async-done(((bf16[768,512]{1,0:T(8,128)(2,1)}), bf16[384,512]{1,0:T(8,128)(2,1)}) %reduce-scatter.4.cloned.1.call-update) | async-done | bytes 393232
  (73 shorter events, 59.7 us)
Async XLA Ops:
  6.5 3.8 %copy-start = (bf16[3,768,384]{2,1,0:T(8,128)(2,1)S(1)}, bf16[3,768,384]{2,1,0:T(8,128)(2,1)}, u32[]{:S(2)}) copy-start(bf16[3,768,384]{2,1,0:T(8,128)(2,1)} %param.9) | copy-start | bytes 5308420
  6.5 3.5 %copy-start.3 = (f32[768]{0:T(1024)S(1)}, f32[768]{0:T(1024)}, u32[]{:S(2)}) copy-start(f32[768]{0:T(1024)} %param.8) | copy-start | bytes 9220
  11.6 1.0 copy-start.2
  13.5 1.0 copy-start.1
  34.5 39.3 %all-to-all-start = ((bf16[3,2,4,64,384]{4,2,1,0,3:T(4,128)(2,1)}), bf16[3,2,4,64,384]{4,2,1,0,3:T(4,128)(2,1)}, u32[]{:S(2)}, u32[]{:S(2)}) async-start(bf16[3,2,4,64,384]{4,2,1,0,3:T(4,128)(2,1)} %copy-done.1), calls=%async_computation | async-start | bytes 2359296 | tf_op jit(solution)/shard_map/all_to_all | solution.py:54
  73.8 30.1 %all-to-all-start.3 = ((bf16[4,4,32,384]{3,2,1,0:T(8,128)(2,1)}), bf16[4,4,32,384]{3,2,1,0:T(8,128)(2,1)}, u32[]{:S(2)}, u32[]{:S(2)}) async-start(bf16[4,4,32,384]{3,2,1,0:T(8,128)(2,1)} %copy.158), calls=%async_computation.3 | async-start | bytes 786432 | tf_op jit(solution)/shard_map/all_to_all | solution.py:59
  103.8 22.7 %all-to-all-start.1 = ((bf16[2,16,16,384]{3,2,0,1:T(8,128)(2,1)}), bf16[2,16,16,384]{3,2,0,1:T(8,128)(2,1)}, u32[]{:S(2)}, u32[]{:S(2)}) async-start(bf16[2,16,16,384]{3,2,0,1:T(8,128)(2,1)} %copy.140), calls=%async_computation.1 | async-start | bytes 786432 | tf_op jit(solution)/shard_map/all_to_all | solution.py:56
  108.9 37.8 %all-gather.9.cloned.1.call-start = ((), (), s32[]{:S(2)}) async-start(), calls=%async_computation.7 | async-start | bytes 4718592 | tf_op jit(solution)/shard_map/all_gather | solution.py:65
  132.6 67.3 %all-gather.5.cloned.1.call-start = ((), (), s32[]{:S(2)}) async-start(), calls=%async_computation.5 | async-start | bytes 2949120 | tf_op jit(solution)/shard_map/all_gather | solution.py:71
  133.4 117.5 %all-gather.7.cloned.1.call-start = ((), (), s32[]{:S(2)}) async-start(), calls=%async_computation.6 | async-start | bytes 2949120 | tf_op jit(solution)/shard_map/all_gather | solution.py:75
  134.1 136.6 %reduce-scatter.4.cloned.1.call-start = ((), (), s32[]{:S(2)}) async-start(), calls=%async_computation.8 | async-start | bytes 1179648
  153.7 97.2 %copy-start.4 = (f32[768]{0:T(1024)S(1)}, f32[768]{0:T(1024)}, u32[]{:S(2)}) copy-start(f32[768]{0:T(1024)} %param.11) | copy-start | bytes 9220
Sparse Core Ops, SparseCore 0:
  132.8 13.9 all-gather.8
  148.3 51.6 all-gather.4
  201.6 49.2 all-gather.6
  263.6 7.0 reduce-scatter.3
